TPU v7x, 32 devices: a whole 2x2x4 slice. The times are simulated.
32 devices in a mesh: tok: 16 (over z, y, core), feat: 2 (over x).
Axes of the slice: x: 2, y: 2, z: 4, core: 2. Of those that a mesh axis runs over, the one named last changes fastest.
Arguments:
- activations: bfloat16 [8192, 16384], P('tok', 'feat'), may hold values from -300 to 300
- down_proj: bfloat16 [16384, 1024], P('feat', 'tok'), may hold values from -0.00048828125 to 0.00048828125
- precond: bfloat16 [1024, 1024], replicated, may hold values from -1 to 2, as said below
- target: bfloat16 [8192, 256], P('tok'), may hold values from -8 to 8
Outputs:
- solution: float32 [1024, 256], P('feat')
- residual: float32 [8192, 256], P('tok')
Inputs may be any that keep to these rules, and one draw needn't show every extreme that they name: `precond`: upper triangular.
All inputs are finite; a program needn't handle non-finite values.
Results may differ from a plain program's by a relative error of at most 0.025.
Values may be sent and summed in bfloat16 or wider, within the bound.
A program may use at most 64 MiB of HBM per device.

v0:
```python
import jax
import jax.numpy as jnp
from jax import lax
from jax.sharding import PartitionSpec as P

ITERS = 2


precise = lax.Precision.HIGHEST


def solve_gram(matrix, right):
    lower = jnp.linalg.cholesky(matrix)
    middle = lax.linalg.triangular_solve(lower, right, left_side=True, lower=True)
    return lax.linalg.triangular_solve(lower, middle, left_side=True, lower=True, transpose_a=True)


def on_device(activations, down_proj, precond, target):
    feat_count = lax.axis_size("feat")
    feat_index = lax.axis_index("feat")
    share_rows = precond.shape[0] // feat_count
    partial_map = jnp.dot(
        activations,
        lax.all_gather(down_proj, "tok", axis=1, tiled=True),
        preferred_element_type=jnp.float32,
    )
    joined_share = lax.psum_scatter(partial_map, "feat", scatter_dimension=1, tiled=True).astype(
        jnp.bfloat16
    )
    row_block = lax.dynamic_slice_in_dim(precond, feat_index * share_rows, share_rows, 0)
    col_block = lax.dynamic_slice_in_dim(precond, feat_index * share_rows, share_rows, 1)

    def gradient(current):
        partial_back = lax.dot_general(
            joined_share,
            current.astype(jnp.bfloat16),
            (((0,), (0,)), ((), ())),
            preferred_element_type=jnp.float32,
        )
        summed = lax.psum(partial_back, "tok")
        gathered = lax.all_gather(summed.astype(jnp.bfloat16), "feat", axis=0, tiled=True)
        descent = lax.dot_general(
            col_block, gathered, (((0,), (0,)), ((), ())), preferred_element_type=jnp.float32
        )
        gram_matrix = lax.psum(jnp.dot(descent.T, descent, precision=precise), "feat")
        return (descent, gram_matrix)

    residual = target.astype(jnp.float32)
    descent, gram_now = gradient(residual)
    direction = descent
    solution = jnp.zeros((share_rows, target.shape[1]), jnp.float32)
    for iteration in range(ITERS):
        rounded_dir = lax.all_gather(direction.astype(jnp.bfloat16), "feat", axis=0, tiled=True)
        lift_rows = jnp.dot(row_block, rounded_dir, preferred_element_type=jnp.float32)
        partial_image = jnp.dot(
            joined_share, lift_rows.astype(jnp.bfloat16), preferred_element_type=jnp.float32
        )
        image_now = lax.psum(partial_image, "feat")
        curvature = lax.psum(jnp.dot(image_now.T, image_now, precision=precise), "tok")
        step_size = solve_gram(curvature, gram_now)
        solution = solution + jnp.dot(lift_rows, step_size, precision=precise)
        residual = residual - jnp.dot(image_now, step_size, precision=precise)
        if iteration + 1 < ITERS:
            descent, gram_next = gradient(residual)
            mixing = solve_gram(gram_now, gram_next)
            direction = descent + jnp.dot(direction, mixing, precision=precise)
            gram_now = gram_next
    return (solution, residual)


def solution(mesh):
    placed = (P("tok", "feat"), P("feat", "tok"), P(), P("tok", None))
    return jax.shard_map(
        on_device,
        mesh=mesh,
        in_specs=placed,
        out_specs=(P("feat", None), P("tok", None)),
        check_vma=False,
    )
```

profile of v0, /device:TPU:0, one launch (start us, length us, event | category | flops | bytes accessed | tf_op | source)
XLA Modules:
  0.0 793.8 jit_solution(5459391959284262204)
XLA Ops:
  8.0 131.8 %all-gather.2.cloned.1.call-done = bf16[8192,1024]{0,1:T(8,128)(2,1)} async-done(((bf16[8192,64]{0,1:T(8,128)(2,1)}), bf16[8192,1024]{0,1:T(8,128)(2,1)}) %all-gather.2.cloned.1.call-update) | async-done | bytes 16777232 | tf_op jit(solution)/shard_map/all_gather | solution.py:24
  139.8 15.8 %fusion.65 = f32[512,1024]{1,0:T(8,128)} fusion(bf16[512,8192]{1,0:T(8,128)(2,1)} %param.9, bf16[8192,1024]{0,1:T(8,128)(2,1)} %all-gather.2.cloned.1.call-done), kind=kOutput, calls=%fused_computation.123 | convolution fusion | flops 8589934592 | bytes 27262976 | tf_op jit(solution)/shard_map/dot_general | solution.py:22
  155.7 30.1 %reduce-scatter.2.cloned.1.call-done = f32[512,512]{1,0:T(8,128)} async-done(((f32[512,1024]{1,0:T(8,128)}), f32[512,512]{1,0:T(8,128)}) %reduce-scatter.2.cloned.1.call-update) | async-done | bytes 1048592 | tf_op jit(solution)/shard_map/reduce_scatter | solution.py:27
  187.5 66.5 %all-reduce.19 = bf16[512,256]{1,0:T(8,128)(2,1)S(1)} all-reduce(f32[512,256]{1,0:T(8,128)S(1)} %fusion.66), channel_id=1, replica_groups=mesh['tok'=16,'feat'=2] {'tok'}, use_global_device_ids=true, to_apply=%region_1.0 | all-reduce | flops 131072 | bytes 786432 | tf_op jit(solution)/shard_map/psum | solution.py:40
  254.0 9.1 %all_gather.16 = bf16[1024,256]{1,0:T(8,128)(2,1)S(1)} all-gather(bf16[512,256]{1,0:T(8,128)(2,1)S(1)} %all-reduce.19), channel_id=1, replica_groups=mesh['tok'=16,'feat'=2] {'feat'}, dimensions={0}, use_global_device_ids=true | all-gather | bytes 786432 | tf_op jit(solution)/shard_map/all_gather | solution.py:41
  263.7 7.0 all_gather.17
  274.0 32.3 %all-reduce.18.cloned.1.call-done = (f32[256,256]{0,1:T(8,128)}, f32[512,256]{1,0:T(8,128)}) async-done(((f32[256,256]{0,1:T(8,128)}, f32[512,256]{1,0:T(8,128)}), (f32[256,256]{0,1:T(8,128)}, f32[512,256]{1,0:T(8,128)})) %all-reduce.18.cloned.1.call-update) | async-done | bytes 786448 | tf_op jit(solution)/shard_map/psum | solution.py:45
  306.3 2.9 fusion.67
  310.7 11.7 %cholesky.206 = f32[128,128]{1,0:T(8,128)S(1)} custom-call(f32[128,128]{1,0:T(8,128)S(1)} %cholesky.273), custom_call_target="Cholesky" | custom-call | tf_op jit(solution)/shard_map/jit(cholesky)/cholesky | solution.py:13
  322.5 9.8 %custom-call.23 = f32[1,128,128]{1,2,0:T(8,128)S(1)} custom-call(f32[1,128,128]{2,1,0:T(8,128)S(1)} %get-tuple-element.90), custom_call_target="InvertDiagBlocksLowerTriangular" | custom-call | tf_op jit(solution)/shard_map/jit(cholesky)/cholesky | solution.py:13
  332.8 11.7 %cholesky.223 = f32[128,128]{1,0:T(8,128)S(1)} custom-call(f32[128,128]{1,0:T(8,128)S(1)} %convolution_subtract_fusion.9), custom_call_target="Cholesky" | custom-call | tf_op jit(solution)/shard_map/jit(cholesky)/cholesky | solution.py:13
  346.5 52.8 %all-reduce.10.cloned.1.call-done = f32[256,256]{0,1:T(8,128)} async-done(((f32[256,256]{0,1:T(8,128)}), f32[256,256]{0,1:T(8,128)}) %all-reduce.10.cloned.1.call-update) | async-done | bytes 262160 | tf_op jit(solution)/shard_map/psum | solution.py:59
  402.1 12.1 %cholesky.172 = f32[128,128]{1,0:T(8,128)S(1)} custom-call(f32[128,128]{1,0:T(8,128)S(1)} %cholesky.270), custom_call_target="Cholesky" | custom-call | tf_op jit(solution)/shard_map/jit(cholesky)/cholesky | solution.py:13
  414.2 9.8 %custom-call.20 = f32[1,128,128]{1,2,0:T(8,128)S(1)} custom-call(f32[1,128,128]{2,1,0:T(8,128)S(1)} %get-tuple-element.94), custom_call_target="InvertDiagBlocksLowerTriangular" | custom-call | tf_op jit(solution)/shard_map/jit(cholesky)/cholesky | solution.py:13
  426.2 11.7 %cholesky.189 = f32[128,128]{1,0:T(8,128)S(1)} custom-call(f32[128,128]{1,0:T(8,128)S(1)} %convolution_subtract_fusion.10), custom_call_target="Cholesky" | custom-call | tf_op jit(solution)/shard_map/jit(cholesky)/cholesky | solution.py:13
  441.1 4.2 while.12
  446.0 20.5 %custom-call.22 = f32[2,128,128]{1,2,0:T(8,128)S(1)} custom-call(f32[2,128,128]{2,1,0:T(8,128)} %copy-done.22), custom_call_target="InvertDiagBlocksLowerTriangular" | custom-call | tf_op jit(solution)/shard_map/triangular_solve/custom-call.4 | solution.py:15
  473.5 66.3 %all-reduce.20 = bf16[512,256]{1,0:T(8,128)(2,1)} all-reduce(f32[512,256]{1,0:T(8,128)} %fusion.17), channel_id=1, replica_groups=mesh['tok'=16,'feat'=2] {'tok'}, use_global_device_ids=true, to_apply=%region_9.13 | all-reduce | flops 131072 | bytes 786432 | tf_op jit(solution)/shard_map/psum | solution.py:40
  539.8 7.2 all_gather.18
  550.8 4.8 while.13
  551.4 1.8 bitcast_dynamic-update-slice_fusion.7
  553.7 1.8 bitcast_dynamic-update-slice_fusion.7
  555.6 21.1 %custom-call.25 = f32[2,128,128]{1,2,0:T(8,128)} custom-call(f32[2,128,128]{2,1,0:T(8,128)} %get-tuple-element.48), custom_call_target="InvertDiagBlocksLowerTriangular" | custom-call | tf_op jit(solution)/shard_map/triangular_solve/custom-call.4 | solution.py:15
  583.5 7.0 all_gather.19
  593.2 29.1 %all-reduce.14.cloned.1.call-done = f32[512,256]{1,0:T(8,128)} async-done(((f32[512,256]{1,0:T(8,128)}), f32[512,256]{1,0:T(8,128)}) %all-reduce.14.cloned.1.call-update) | async-done | bytes 524304 | tf_op jit(solution)/shard_map/psum | solution.py:58
  622.3 2.9 fusion.70
  626.6 87.8 %all-reduce.16.cloned.1.call-done = f32[256,256]{0,1:T(8,128)} async-done(((f32[256,256]{0,1:T(8,128)}), f32[256,256]{0,1:T(8,128)}) %all-reduce.16.cloned.1.call-update) | async-done | bytes 262160 | tf_op jit(solution)/shard_map/psum | solution.py:59
  716.6 11.7 %cholesky.240 = f32[128,128]{1,0:T(8,128)S(1)} custom-call(f32[128,128]{1,0:T(8,128)S(1)} %cholesky.276), custom_call_target="Cholesky" | custom-call | tf_op jit(solution)/shard_map/jit(cholesky)/cholesky | solution.py:13
  728.3 9.8 %custom-call.26 = f32[1,128,128]{1,2,0:T(8,128)S(1)} custom-call(f32[1,128,128]{2,1,0:T(8,128)S(1)} %get-tuple-element.86), custom_call_target="InvertDiagBlocksLowerTriangular" | custom-call | tf_op jit(solution)/shard_map/jit(cholesky)/cholesky | solution.py:13
  739.5 11.7 %cholesky.257 = f32[128,128]{1,0:T(8,128)S(1)} custom-call(f32[128,128]{1,0:T(8,128)S(1)} %convolution_subtract_fusion.8), custom_call_target="Cholesky" | custom-call | tf_op jit(solution)/shard_map/jit(cholesky)/cholesky | solution.py:13
  754.8 4.2 while.14
  759.6 20.5 %custom-call.28 = f32[2,128,128]{1,2,0:T(8,128)S(1)} custom-call(f32[2,128,128]{2,1,0:T(8,128)} %copy-done.21), custom_call_target="InvertDiagBlocksLowerTriangular" | custom-call | tf_op jit(solution)/shard_map/triangular_solve/custom-call.4 | solution.py:15
  (147 shorter events, 59.6 us)
Async XLA Ops:
  7.2 256.0 %copy-start = (bf16[1024,1024]{1,0:T(8,128)(2,1)S(1)}, bf16[1024,1024]{1,0:T(8,128)(2,1)}, u32[]{:S(2)}) copy-start(bf16[1024,1024]{1,0:T(8,128)(2,1)} %param.11) | copy-start | bytes 6291460
  7.2 132.6 %all-gather.2.cloned.1.call-start = ((), (), s32[]{:S(2)}) async-start(), calls=%async_computation.1 | async-start | bytes 17825792 | tf_op jit(solution)/shard_map/all_gather | solution.py:24
  7.9 177.9 %reduce-scatter.2.cloned.1.call-start = ((), (), s32[]{:S(2)}) async-start(), calls=%async_computation.2 | async-start | bytes 3145728 | tf_op jit(solution)/shard_map/reduce_scatter | solution.py:27
  155.6 31.5 %copy-start.16 = (bf16[512,256]{1,0:T(8,128)(2,1)S(1)}, bf16[512,256]{1,0:T(8,128)(2,1)}, u32[]{:S(2)}) copy-start(bf16[512,256]{1,0:T(8,128)(2,1)} %param.12) | copy-start | bytes 786436
  155.7 150.7 %all-reduce.18.cloned.1.call-start = ((), (), s32[]{:S(2)}) async-start(), calls=%async_computation.7 | async-start | bytes 1572864 | tf_op jit(solution)/shard_map/psum | solution.py:45
  263.6 9.2 %copy-start.5 = (f32[512,256]{1,0:T(8,128)}, f32[512,256]{1,0:T(8,128)S(1)}, u32[]{:S(2)}) copy-start(f32[512,256]{1,0:T(8,128)S(1)} %get-tuple-element.96) | copy-start | bytes 1572868
  271.1 1.7 copy-start.3
  274.0 125.3 %all-reduce.10.cloned.1.call-start = ((), (), s32[]{:S(2)}) async-start(), calls=%async_computation.3 | async-start | bytes 524288 | tf_op jit(solution)/shard_map/psum | solution.py:59
  306.3 4.3 copy-start.10
  309.3 267.4 %all-reduce.12.cloned.1.call-start = ((), (), s32[]{:S(2)}) async-start(), calls=%async_computation.4 | async-start | bytes 524288 | tf_op jit(solution)/shard_map/psum | solution.py:45
  401.4 0.7 copy-start.18
  438.0 2.0 copy-start.14
  445.3 0.7 copy-start.22
  466.5 0.7 copy-start.20
  466.5 4.2 copy-start.17
  470.1 0.7 copy-start.12
  547.5 0.8 copy-start.8
  550.1 72.2 %all-reduce.14.cloned.1.call-start = ((), (), s32[]{:S(2)}) async-start(), calls=%async_computation.5 | async-start | bytes 1048576 | tf_op jit(solution)/shard_map/psum | solution.py:58
  576.7 6.2 copy-start.6
  576.7 6.2 copy-start.9
  591.0 0.8 copy-start.1
  591.8 33.4 %copy-start.13 = (f32[128,256]{1,0:T(8,128)S(1)}, f32[128,256]{1,0:T(8,128)}, u32[]{:S(2)}) copy-start(f32[128,256]{1,0:T(8,128)} %copy-done.12) | copy-start | bytes 393220
  592.9 32.4 %copy-start.4 = (f32[512,256]{1,0:T(8,128)S(1)}, f32[512,256]{1,0:T(8,128)}, u32[]{:S(2)}) copy-start(f32[512,256]{1,0:T(8,128)} %copy-done.3) | copy-start | bytes 1572868
  592.9 121.5 %all-reduce.16.cloned.1.call-start = ((), (), s32[]{:S(2)}) async-start(), calls=%async_computation.6 | async-start | bytes 524288 | tf_op jit(solution)/shard_map/psum | solution.py:59
  716.5 21.6 %copy-start.19 = (f32[256,256]{1,0:T(8,128)}, f32[256,256]{1,0:T(8,128)S(1)}, u32[]{:S(2)}) copy-start(f32[256,256]{1,0:T(8,128)S(1)} %fusion.12) | copy-start | bytes 786436
  738.4 45.4 %copy-start.2 = (f32[512,256]{1,0:T(8,128)S(1)}, f32[512,256]{1,0:T(8,128)}, u32[]{:S(2)}) copy-start(f32[512,256]{1,0:T(8,128)} %copy-done.1) | copy-start | bytes 1572868
  752.0 1.8 copy-start.15
  759.0 0.6 copy-start.21
  780.1 3.7 copy-start.11
  780.1 5.1 copy-start.7
Sparse Core Ops, SparseCore 0:
  10.2 129.5 all-gather.1
  155.8 29.9 reduce-scatter.1
  274.1 32.1 all-reduce.17
  310.1 89.1 all-reduce.9
  550.2 22.3 all-reduce.11
  593.1 29.2 all-reduce.13
  625.7 88.7 all-reduce.15
where the time goes:
time: 801 us; the launch traced here: 794 us
  waiting for transfers between devices  365 us (46%)
  other arithmetic  170 us (21%)
  blocking collectives  163 us (20%)
  matrix products  54.2 us (7%)
  local copies, waits for them, and re-layouts  21 us (3%)
  between operations  18.9 us (2%)
    psum x2, waiting for transfers between devices, on_device(): lax.psum(jnp.dot(image_now.T, image_now, precision=precise), 'tok')  141 us
    psum x2, blocking collectives, gradient(): summed = lax.psum(partial_back, 'tok')  133 us
    all_gather x1, waiting for transfers between devices, on_device(): lax.all_gather(down_proj, 'tok', axis=1, tiled=True)  132 us
    another operation x19, other arithmetic, solve_gram(): lower = jnp.linalg.cholesky(matrix)  103 us
    another operation x7, other arithmetic, solve_gram(): lax.linalg.triangular_solve(lower, middle, left_side=True, lower=True, tr...  64.1 us
    psum x2, waiting for transfers between devices, gradient(): lax.psum(jnp.dot(descent.T, descent, precision=precise), 'feat')  32.3 us
    reduce_scatter x1, waiting for transfers between devices, on_device(): lax.psum_scatter(partial_map, 'feat', scatter_dimension=1, tiled=True)  30.1 us
    psum x1, waiting for transfers between devices, on_device(): image_now = lax.psum(partial_image, 'feat')  29.1 us
  transfers between devices with their start and end apart: 7, of which 6 were waited for; matrix products, arithmetic and copies ran while one was open for 8% of the time, Pallas kernels for 0%

commit v1 on v0

--- a/solution.py
+++ b/solution.py
@@ -1,18 +1,306 @@
+import functools
+
 import jax
 import jax.numpy as jnp
 from jax import lax
+from jax.experimental import pallas as pl
+from jax.experimental.pallas import tpu as pltpu
 from jax.sharding import PartitionSpec as P
 
 ITERS = 2
-
-
+Z, Y, CORES = 4, 2, 2
+BLOCK = 256
+DEPTH = 1024
+MESH = pl.DeviceIdType.MESH
 precise = lax.Precision.HIGHEST
+
+
+def spread(buf, send, recv, on_slab):
+    me = lax.axis_index("tok")
+    z, y, c = me // (Y * CORES), (me // CORES) % Y, me % CORES
+
+    def index(zz, yy, cc):
+        return (zz * Y + yy) * CORES + cc
+
+    targets = (me + Y * CORES, me - Y * CORES, index(z, 1 - y, c), index(z, y, 1 - c))
+
+    def copy(i, way):
+        return pltpu.make_async_remote_copy(
+            src_ref=buf.at[i],
+            dst_ref=buf.at[i],
+            send_sem=send.at[way, i],
+            recv_sem=recv.at[i],
+            device_id={"tok": targets[way]},
+            device_id_type=MESH,
+        )
+
+    def along(distance, visit):
+        for sign in (1, -1) if distance else (1,):
+            zz = z + sign * distance
+
+            @pl.when((zz >= 0) & (zz < Z))
+            def _():
+                visit(zz, sign)
+
+    def onward(i, zz, sign, act):
+        if sign != 1 or zz is z:
+
+            @pl.when(z < Z - 1)
+            def _():
+                act(copy(i, 0))
+
+        if sign == 1:
+
+            @pl.when(z > 0)
+            def _():
+                act(copy(i, 1))
+
+        act(copy(i, 2))
+        act(copy(i, 3))
+
+    onward(me, z, 1, lambda k: k.start())
+    for stage in range(Z):
+
+        def line(zz, sign):
+            i = index(zz, y, c)
+            copy(i, 2).wait_recv()
+            onward(i, zz, sign, lambda k: k.start())
+
+        def side(zz, sign):
+            i = index(zz, 1 - y, c)
+            copy(i, 2).wait_recv()
+            copy(i, 3).start()
+
+        def slab(zz, sign):
+            copy(index(zz, y, 1 - c), 3).wait_recv()
+            copy(index(zz, 1 - y, 1 - c), 3).wait_recv()
+            if on_slab is not None:
+                on_slab(zz)
+
+        if stage + 1 < Z:
+            along(stage + 1, line)
+        along(stage, side)
+        along(stage, slab)
+
+    onward(me, z, 1, lambda k: k.wait_send())
+    for stage in range(Z):
+        if stage:
+            along(stage, lambda zz, sign: onward(index(zz, y, c), zz, sign, lambda k: k.wait_send()))
+        along(stage, lambda zz, sign: copy(index(zz, 1 - y, c), 3).wait_send())
+
+
+def pairs(slabs):
+    upper = [(i, j) for i in range(slabs) for j in range(i, slabs)]
+    return upper + [(i, None) for i in range(slabs)]
+
+
+def reduce_kernel(
+    a_ref, d_ref, t_ref, j_ref, m_ref,
+    a_buf, d_buf, total, mine, theirs, out_buf, in_buf, all_buf,
+    a_sem, d_sem, d_send, d_recv, x_send, x_recv, r_send, r_recv, p_send, p_recv, m_send, m_recv,
+):
+    me, feat = lax.axis_index("tok"), lax.axis_index("feat")
+    count = Z * Y * CORES
+    group = Y * CORES
+
+    load_a = pltpu.make_async_copy(a_ref, a_buf, a_sem)
+    load_d = pltpu.make_async_copy(d_ref, d_buf.at[me], d_sem)
+    load_d.start()
+    load_a.start()
+
+    barrier = pltpu.get_barrier_semaphore()
+    for step in range(1, count):
+        pl.semaphore_signal(
+            barrier, inc=1, device_id={"tok": lax.rem(me + step, count)}, device_id_type=MESH
+        )
+    pl.semaphore_signal(barrier, inc=1, device_id={"feat": 1 - feat}, device_id_type=MESH)
+    pl.semaphore_wait(barrier, count)
+    load_d.wait()
+
+    def swap(slab):
+        return pltpu.make_async_remote_copy(
+            src_ref=mine.at[slab],
+            dst_ref=theirs.at[slab],
+            send_sem=x_send.at[slab],
+            recv_sem=x_recv.at[slab],
+            device_id={"feat": 1 - feat},
+            device_id_type=MESH,
+        )
+
+    def project(slab):
+        total[...] = jnp.zeros_like(total)
+
+        def part(k, carry):
+            columns = pl.ds(pl.multiple_of(k * DEPTH, DEPTH), DEPTH)
+            weights = d_buf[pl.ds(slab * group, group), :, columns].reshape(BLOCK, DEPTH)
+            total[...] += lax.dot_general(
+                a_buf[:, columns], weights, (((1,), (1,)), ((), ())), preferred_element_type=jnp.float32
+            )
+            return carry
+
+        lax.fori_loop(0, a_buf.shape[1] // DEPTH, part, 0)
+        mine[slab] = total[...].astype(jnp.bfloat16)
+        swap(slab).start()
+
+    load_a.wait()
+    spread(d_buf, d_send, d_recv, project)
+    for slab in range(Z):
+        swap(slab).wait()
+        j_ref[slab] = (mine[slab].astype(jnp.float32) + theirs[slab].astype(jnp.float32)).astype(
+            jnp.bfloat16
+        )
+
+    blocks = pairs(Z)
+    half = len(blocks) // 2
+    rows = BLOCK // count
+    for owner in range(2):
+
+        @pl.when(feat == owner)
+        def _():
+            for n, (i, j) in enumerate(blocks[owner * half : (owner + 1) * half]):
+                product = lax.dot_general(
+                    j_ref[i],
+                    t_ref[...] if j is None else j_ref[j],
+                    (((0,), (0,)), ((), ())),
+                    preferred_element_type=jnp.float32,
+                )
+                out_buf[:, n] = product.astype(jnp.bfloat16).reshape(count, rows, BLOCK)
+
+    def send_part(step):
+        other = lax.rem(me + step, count)
+        return pltpu.make_async_remote_copy(
+            src_ref=out_buf.at[other],
+            dst_ref=in_buf.at[me],
+            send_sem=r_send.at[step],
+            recv_sem=r_recv.at[me],
+            device_id={"tok": other},
+            device_id_type=MESH,
+        )
+
+    def take_part(step):
+        other = lax.rem(me + step, count)
+        pltpu.make_async_remote_copy(
+            src_ref=out_buf.at[other],
+            dst_ref=in_buf.at[other],
+            send_sem=r_send.at[step],
+            recv_sem=r_recv.at[other],
+            device_id={"tok": other},
+            device_id_type=MESH,
+        ).wait_recv()
+
+    for step in range(1, count):
+        send_part(step).start()
+    in_buf[me] = out_buf[me]
+    for step in range(1, count):
+        take_part(step)
+    for n in range(half):
+        summed = in_buf[0, n].astype(jnp.float32)
+        for i in range(1, count):
+            summed += in_buf[i, n].astype(jnp.float32)
+        all_buf[me, feat * half + n] = summed.astype(jnp.bfloat16)
+    own = all_buf.at[me, pl.ds(feat * half, half)]
+    across = pltpu.make_async_remote_copy(
+        src_ref=own, dst_ref=own, send_sem=p_send, recv_sem=p_recv,
+        device_id={"feat": 1 - feat}, device_id_type=MESH,
+    )
+    across.start()
+    across.wait()
+    spread(all_buf, m_send, m_recv, None)
+    for step in range(1, count):
+        send_part(step).wait_send()
+    for i in range(count):
+        m_ref[:, pl.ds(i * rows, rows), :] = all_buf[i]
+
+
+def reduced(activations, down_rows, target):
+    count = Z * Y * CORES
+    tokens, features = activations.shape
+    share = down_rows.shape[0]
+    blocks = len(pairs(Z))
+    half, rows = blocks // 2, BLOCK // count
+    dma = pltpu.SemaphoreType.DMA
+    bf16 = jnp.bfloat16
+    whole = pl.BlockSpec(memory_space=pltpu.VMEM)
+    return pl.pallas_call(
+        reduce_kernel,
+        out_shape=(
+            jax.ShapeDtypeStruct((Z, tokens, BLOCK), bf16),
+            jax.ShapeDtypeStruct((blocks, BLOCK, BLOCK), bf16),
+        ),
+        in_specs=[pl.BlockSpec(memory_space=pl.ANY)] * 2 + [whole],
+        out_specs=(whole, whole),
+        scratch_shapes=[
+            pltpu.VMEM((tokens, features), bf16),
+            pltpu.VMEM((count, share, features), bf16),
+            pltpu.VMEM((tokens, BLOCK), jnp.float32),
+            pltpu.VMEM((Z, tokens, BLOCK), bf16),
+            pltpu.VMEM((Z, tokens, BLOCK), bf16),
+            pltpu.VMEM((count, half, rows, BLOCK), bf16),
+            pltpu.VMEM((count, half, rows, BLOCK), bf16),
+            pltpu.VMEM((count, blocks, rows, BLOCK), bf16),
+            dma, dma, dma((4, count)), dma((count,)), dma((Z,)), dma((Z,)),
+            dma((count,)), dma((count,)), dma, dma, dma((4, count)), dma((count,)),
+        ],
+        compiler_params=pltpu.CompilerParams(
+            collective_id=0, has_side_effects=True, vmem_limit_bytes=56 * 2**20
+        ),
+        cost_estimate=pl.CostEstimate(
+            flops=2 * tokens * features * share * count, bytes_accessed=2 * tokens * features, transcendentals=0
+        ),
+    )(activations, down_rows, target)
 
 
 def solve_gram(matrix, right):
     lower = jnp.linalg.cholesky(matrix)
     middle = lax.linalg.triangular_solve(lower, right, left_side=True, lower=True)
     return lax.linalg.triangular_solve(lower, middle, left_side=True, lower=True, transpose_a=True)
+
+
+def wide_dot(a, b, dims):
+    return lax.dot_general(a, b, (dims, ((), ())), preferred_element_type=jnp.float32)
+
+
+def on_block(activations, down_proj, precond, target):
+    feat_index = lax.axis_index("feat")
+    joined, sums = reduced(activations, down_proj.T, target)
+    blocks = dict(zip(pairs(Z), sums))
+    normal = jnp.concatenate(
+        [
+            jnp.concatenate([blocks[i, j] if i <= j else blocks[j, i].T for j in range(Z)], axis=1)
+            for i in range(Z)
+        ],
+        axis=0,
+    )
+    back = jnp.concatenate([blocks[i, None] for i in range(Z)], axis=0).astype(jnp.float32)
+
+    def gradient(current):
+        descent = wide_dot(precond, current.astype(jnp.bfloat16), ((0,), (0,)))
+        return descent, jnp.dot(descent.T, descent, precision=precise)
+
+    descent, gram_now = gradient(back)
+    direction = descent
+    answer = jnp.zeros(back.shape, jnp.float32)
+    for iteration in range(ITERS):
+        lift = wide_dot(precond, direction.astype(jnp.bfloat16), ((1,), (0,)))
+        rounded = lift.astype(jnp.bfloat16)
+        pushed = wide_dot(normal, rounded, ((1,), (0,)))
+        curvature = jnp.dot(rounded.astype(jnp.float32).T, pushed, precision=precise)
+        curvature = 0.5 * (curvature + curvature.T)
+        step_size = solve_gram(curvature, gram_now)
+        answer = answer + jnp.dot(lift, step_size, precision=precise)
+        if iteration + 1 < ITERS:
+            back = back - jnp.dot(pushed, step_size, precision=precise)
+            descent, gram_next = gradient(back)
+            mixing = solve_gram(gram_now, gram_next)
+            direction = descent + jnp.dot(direction, mixing, precision=precise)
+            gram_now = gram_next
+    rounded = answer.astype(jnp.bfloat16).reshape(Z, BLOCK, -1)
+    fitted = sum(wide_dot(joined[i], rounded[i], ((1,), (0,))) for i in range(Z))
+    share = answer.shape[0] // lax.axis_size("feat")
+    return (
+        lax.dynamic_slice_in_dim(answer, feat_index * share, share, 0),
+        target.astype(jnp.float32) - fitted,
+    )
 
 
 def on_device(activations, down_proj, precond, target):
@@ -69,9 +357,10 @@
 
 
 def solution(mesh):
+    small = mesh.shape["tok"] == Z * Y * CORES and mesh.shape["feat"] == 2
     placed = (P("tok", "feat"), P("feat", "tok"), P(), P("tok", None))
     return jax.shard_map(
-        on_device,
+        on_block if small else on_device,
         mesh=mesh,
         in_specs=placed,
         out_specs=(P("feat", None), P("tok", None)),

time: 801 us -> 469 us (0.59)
  waiting for transfers between devices: 365 us -> 0 us
  blocking collectives: 163 us -> 0 us
  Pallas kernels: 0 us -> 160 us
  local copies, waits for them, and re-layouts: 21 us -> 56.1 us
  other arithmetic: 170 us -> 200 us
  between operations: 18.9 us -> 5.47 us
  matrix products: 54.2 us -> 41.2 us
    psum x5 -> x0, waiting for transfers between devices: 202 us -> none  [the longest x2 141 us: on_device(): lax.psum(jnp.dot(image_now.T, image_now, precision=precise), 'tok')]
    pallas_call x0 -> x1, Pallas kernels: none -> 160 us  [reduced(): pl.pallas_call(reduce_kernel, out_shape=(jax.ShapeDtypeStruct((Z, tokens,...]
    psum x2 -> x0, blocking collectives: 133 us -> none  [gradient(): summed = lax.psum(partial_back, 'tok')]
    all_gather x1 -> x0, waiting for transfers between devices: 132 us -> none  [on_device(): lax.all_gather(down_proj, 'tok', axis=1, tiled=True)]
    all_gather x4 -> x0, blocking collectives: 30.5 us -> none  [the longest x2 16.4 us: gradient(): lax.all_gather(summed.astype(jnp.bfloat16), 'feat', axis=0, tiled=True)]
    reduce_scatter x1 -> x0, waiting for transfers between devices: 30.1 us -> none  [on_device(): lax.psum_scatter(partial_map, 'feat', scatter_dimension=1, tiled=True)]
    dot_general x18, matrix products: 36.9 us -> 17.7 us  [the longest x10 6.15 us: wide_dot(): lax.dot_general(a, b, (dims, ((), ())), preferred_element_type=jnp.float32)]
    another operation x19, other arithmetic: 103 us -> 119 us  [solve_gram(): lower = jnp.linalg.cholesky(matrix)]
  transfers between devices with their start and end apart: 7 -> 0, of which waited for: 6 -> 0; matrix products, arithmetic and copies ran while one was open for 8% -> 0% of each run, Pallas kernels for 0% -> 0%
where the time goes in v1:
time: 469 us; the launch traced here: 463 us
  other arithmetic  200 us (43%)
  Pallas kernels  160 us (34%)
  local copies, waits for them, and re-layouts  56.1 us (12%)
  matrix products  41.2 us (9%)
  between operations  5.47 us (1%)
    pallas_call x1, Pallas kernels, reduced(): pl.pallas_call(reduce_kernel, out_shape=(jax.ShapeDtypeStruct((Z, tokens,...  160 us
    another operation x19, other arithmetic, solve_gram(): lower = jnp.linalg.cholesky(matrix)  119 us
    another operation x7, other arithmetic, solve_gram(): lax.linalg.triangular_solve(lower, middle, left_side=True, lower=True, tr...  68 us
    another operation x22, local copies, waits for them, and re-layouts, solve_gram(): lax.linalg.triangular_solve(lower, middle, left_side=True, lower=True, tr...  21.4 us
    another operation x6, matrix products, solve_gram(): lower = jnp.linalg.cholesky(matrix)  9.67 us

profile of v1, /device:TPU:0, one launch (start us, length us, event | category | flops | bytes accessed | tf_op | source)
XLA Modules:
  0.0 462.6 jit_solution(17842341977787156894)
XLA Ops:
  0.6 159.7 %shard_map.59 = (bf16[4,512,256]{2,1,0:T(8,128)(2,1)}, bf16[14,256,256]{2,1,0:T(8,128)(2,1)}) custom-call(bf16[512,8192]{1,0:T(8,128)(2,1)} %a_ref.1, bf16[64,8192]{1,0:T(8,128)(2,1)} %bitcast.210, bf16[512,256]{1,0:T(8,128)(2,1)} %t_ref.1), custom_call_target="tpu_custom_call" | custom-call | flops 8589934592 | bytes 8388608 | tf_op jit(solution)/shard_map/pallas_call | solution.py:224
  160.3 2.5 slice_bitcast_fusion.3
  168.5 13.2 %cholesky.206 = f32[128,128]{1,0:T(8,128)} custom-call(f32[128,128]{1,0:T(8,128)} %cholesky.273), custom_call_target="Cholesky" | custom-call | tf_op jit(solution)/shard_map/jit(cholesky)/cholesky | solution.py:254
  183.1 11.3 %custom-call.23 = f32[1,128,128]{1,2,0:T(8,128)} custom-call(f32[1,128,128]{2,1,0:T(8,128)} %get-tuple-element.112), custom_call_target="InvertDiagBlocksLowerTriangular" | custom-call | tf_op jit(solution)/shard_map/jit(cholesky)/cholesky | solution.py:254
  199.4 13.6 %cholesky.223 = f32[128,128]{1,0:T(8,128)} custom-call(f32[128,128]{1,0:T(8,128)} %convolution_subtract_fusion.8), custom_call_target="Cholesky" | custom-call | tf_op jit(solution)/shard_map/jit(cholesky)/cholesky | solution.py:254
  218.9 7.1 %while.13 = (s32[]{:T(128)}, f32[256,256]{1,0:T(8,128)}, s32[2,2]{1,0:T(2,128)S(1)}, f32[2,128,128]{2,1,0:T(8,128)}, s32[]{:T(128)}) while((s32[]{:T(128)}, f32[256,256]{1,0:T(8,128)}, s32[2,2]{1,0:T(2,128)S(1)}, f32[2,128,128]{2,1,0:T(8,128)}, s32[]{:T(128)}) %tuple.98), condition=%wide.while_cond.1.clone, body=%wide.while_body.1.clone.sunk | while | flops 2 | bytes 132705 | solution.py:256
  219.6 2.9 bitcast_dynamic-update-slice_fusion.7
  223.2 2.9 bitcast_dynamic-update-slice_fusion.7
  226.1 21.1 %custom-call.25 = f32[2,128,128]{1,2,0:T(8,128)} custom-call(f32[2,128,128]{2,1,0:T(8,128)} %get-tuple-element.52), custom_call_target="InvertDiagBlocksLowerTriangular" | custom-call | tf_op jit(solution)/shard_map/triangular_solve/custom-call.4 | solution.py:256
  247.2 3.8 copy.6
  253.6 2.0 copy.12
  260.0 6.0 %maximum_maximum_fusion = bf16[1024,1024]{1,0:T(8,128)(2,1)S(1)} fusion(bf16[256,256]{1,0:T(8,128)(2,1)} %get-tuple-element.92, bf16[256,256]{1,0:T(8,128)(2,1)} %copy.11, bf16[256,256]{1,0:T(8,128)(2,1)} %get-tuple-element.102, bf16[256,256]{1,0:T(8,128)(2,1)S(1)} %copy.10, bf16[256,256]{1,0:T(8,128)(2,1)} %get-tuple-element.91, ...), kind=kLoop, calls=%fused_computation.6 | loop fusion | flops 27262976 | bytes 4194304 | tf_op jit(solution)/shard_map/concatenate | solution.py:267
  270.7 1.8 copy.13
  274.3 1.8 copy.14
  277.9 11.7 %cholesky.172 = f32[128,128]{1,0:T(8,128)S(1)} custom-call(f32[128,128]{1,0:T(8,128)S(1)} %cholesky.270), custom_call_target="Cholesky" | custom-call | tf_op jit(solution)/shard_map/jit(cholesky)/cholesky | solution.py:254
  290.3 9.8 %custom-call.20 = f32[1,128,128]{1,2,0:T(8,128)S(1)} custom-call(f32[1,128,128]{2,1,0:T(8,128)S(1)} %get-tuple-element.116), custom_call_target="InvertDiagBlocksLowerTriangular" | custom-call | tf_op jit(solution)/shard_map/jit(cholesky)/cholesky | solution.py:254
  302.9 11.9 %cholesky.189 = f32[128,128]{1,0:T(8,128)S(1)} custom-call(f32[128,128]{1,0:T(8,128)S(1)} %convolution_subtract_fusion.9), custom_call_target="Cholesky" | custom-call | tf_op jit(solution)/shard_map/jit(cholesky)/cholesky | solution.py:254
  319.1 5.7 %while.12 = (s32[]{:T(128)}, f32[256,256]{1,0:T(8,128)}, s32[2,2]{1,0:T(2,128)S(1)}, f32[2,128,128]{2,1,0:T(8,128)S(1)}, s32[]{:T(128)}) while((s32[]{:T(128)}, f32[256,256]{1,0:T(8,128)}, s32[2,2]{1,0:T(2,128)S(1)}, f32[2,128,128]{2,1,0:T(8,128)S(1)}, s32[]{:T(128)}) %tuple.104), condition=%wide.while_cond.1, body=%wide.while_body.1.sunk | while | flops 2 | bytes 131181 | solution.py:256
  319.7 2.3 bitcast_dynamic-update-slice_fusion.6
  322.6 2.2 bitcast_dynamic-update-slice_fusion.6
  325.5 20.5 %custom-call.22 = f32[2,128,128]{1,2,0:T(8,128)S(1)} custom-call(f32[2,128,128]{2,1,0:T(8,128)} %copy-done.18), custom_call_target="InvertDiagBlocksLowerTriangular" | custom-call | tf_op jit(solution)/shard_map/triangular_solve/custom-call.4 | solution.py:256
  360.8 1.8 copy.16
  364.4 1.8 copy.17
  368.6 13.4 %cholesky.240 = f32[128,128]{1,0:T(8,128)} custom-call(f32[128,128]{1,0:T(8,128)} %cholesky.276), custom_call_target="Cholesky" | custom-call | tf_op jit(solution)/shard_map/jit(cholesky)/cholesky | solution.py:254
  385.0 11.3 %custom-call.26 = f32[1,128,128]{1,2,0:T(8,128)} custom-call(f32[1,128,128]{2,1,0:T(8,128)} %get-tuple-element.108), custom_call_target="InvertDiagBlocksLowerTriangular" | custom-call | tf_op jit(solution)/shard_map/jit(cholesky)/cholesky | solution.py:254
  399.7 13.2 %cholesky.257 = f32[128,128]{1,0:T(8,128)} custom-call(f32[128,128]{1,0:T(8,128)} %convolution_subtract_fusion.7), custom_call_target="Cholesky" | custom-call | tf_op jit(solution)/shard_map/jit(cholesky)/cholesky | solution.py:254
  419.4 7.2 %while.14 = (s32[]{:T(128)}, f32[256,256]{1,0:T(8,128)}, s32[2,2]{1,0:T(2,128)S(1)}, f32[2,128,128]{2,1,0:T(8,128)}, s32[]{:T(128)}) while((s32[]{:T(128)}, f32[256,256]{1,0:T(8,128)}, s32[2,2]{1,0:T(2,128)S(1)}, f32[2,128,128]{2,1,0:T(8,128)}, s32[]{:T(128)}) %tuple.105), condition=%wide.while_cond.1.clone.1, body=%wide.while_body.1.clone.1.sunk | while | flops 2 | bytes 132705 | solution.py:256
  420.1 3.0 bitcast_dynamic-update-slice_fusion.8
  423.7 2.9 bitcast_dynamic-update-slice_fusion.8
  426.6 21.3 %custom-call.28 = f32[2,128,128]{1,2,0:T(8,128)} custom-call(f32[2,128,128]{2,1,0:T(8,128)} %get-tuple-element.54), custom_call_target="InvertDiagBlocksLowerTriangular" | custom-call | tf_op jit(solution)/shard_map/triangular_solve/custom-call.4 | solution.py:256
  454.9 1.8 fusion.33
  456.7 2.8 fusion.77
  (142 shorter events, 83.0 us)
Async XLA Ops:
  0.6 162.9 %copy-start = (bf16[1024,1024]{1,0:T(8,128)(2,1)S(1)}, bf16[1024,1024]{1,0:T(8,128)(2,1)}, u32[]{:S(2)}) copy-start(bf16[1024,1024]{1,0:T(8,128)(2,1)} %param.11) | copy-start | bytes 6291460
  162.8 0.7 copy-start.19
  162.8 0.7 copy-start.21
  162.8 1.4 copy-start.23
  162.8 1.4 copy-start.25
  167.1 0.7 copy-start.12
  266.0 1.3 copy-start.1
  267.3 1.0 copy-start.3
  268.3 1.0 copy-start.5
  277.1 0.7 copy-start.10
  324.8 0.7 copy-start.18
  346.0 1.6 copy-start.14
  346.0 5.3 %copy-start.6 = (f32[1024,256]{1,0:T(8,128)S(1)}, f32[1024,256]{1,0:T(8,128)}, u32[]{:S(2)}) copy-start(f32[1024,256]{1,0:T(8,128)} %copy-done.5) | copy-start | bytes 3145732
  346.0 5.3 %copy-start.20 = (bf16[256,256]{1,0:T(8,128)(2,1)S(1)}, bf16[256,256]{1,0:T(8,128)(2,1)}, u32[]{:S(2)}) copy-start(bf16[256,256]{1,0:T(8,128)(2,1)} %copy-done.19) | copy-start | bytes 393220
  346.0 5.3 %copy-start.22 = (bf16[256,256]{1,0:T(8,128)(2,1)S(1)}, bf16[256,256]{1,0:T(8,128)(2,1)}, u32[]{:S(2)}) copy-start(bf16[256,256]{1,0:T(8,128)(2,1)} %copy-done.21) | copy-start | bytes 393220
  346.0 5.3 %copy-start.24 = (bf16[256,256]{1,0:T(8,128)(2,1)S(1)}, bf16[256,256]{1,0:T(8,128)(2,1)}, u32[]{:S(2)}) copy-start(bf16[256,256]{1,0:T(8,128)(2,1)} %copy-done.23) | copy-start | bytes 393220
  346.0 5.3 %copy-start.26 = (bf16[256,256]{1,0:T(8,128)(2,1)S(1)}, bf16[256,256]{1,0:T(8,128)(2,1)}, u32[]{:S(2)}) copy-start(bf16[256,256]{1,0:T(8,128)(2,1)} %copy-done.25) | copy-start | bytes 393220
  351.4 1.0 copy-start.15
  353.1 1.1 copy-start.13
  353.1 1.4 copy-start.8
  357.1 1.6 copy-start.2
  367.2 0.7 copy-start.11
  447.9 6.9 %copy-start.4 = (f32[256,1024]{1,0:T(8,128)S(1)}, f32[256,1024]{1,0:T(8,128)}, u32[]{:S(2)}) copy-start(f32[256,1024]{1,0:T(8,128)} %copy-done.3) | copy-start | bytes 3145732
  447.9 6.9 %copy-start.16 = (f32[128,256]{1,0:T(8,128)S(1)}, f32[128,256]{1,0:T(8,128)}, u32[]{:S(2)}) copy-start(f32[128,256]{1,0:T(8,128)} %copy-done.15) | copy-start | bytes 393220
  456.7 2.8 copy-start.9
  459.5 0.9 copy-start.17
  459.7 1.8 copy-start.7

commit v2 on v1

--- a/solution.py
+++ b/solution.py
@@ -159,8 +159,8 @@
         def _():
             for n, (i, j) in enumerate(blocks[owner * half : (owner + 1) * half]):
                 product = lax.dot_general(
-                    j_ref[i],
-                    t_ref[...] if j is None else j_ref[j],
+                    t_ref[...] if j is None else j_ref[i],
+                    j_ref[i if j is None else j],
                     (((0,), (0,)), ((), ())),
                     preferred_element_type=jnp.float32,
                 )
@@ -250,57 +250,172 @@
     )(activations, down_rows, target)
 
 
+def dot(a, b, dims, precision=None):
+    return lax.dot_general(
+        a, b, (dims, ((), ())), precision=precision, preferred_element_type=jnp.float32
+    )
+
+
+PLAIN, ACROSS = ((1,), (0,)), ((1,), (1,))
+HALF = BLOCK // 2
+
+
+def invert(work, count):
+    height = 8
+    lane = lax.broadcasted_iota(jnp.int32, (1, HALF), 1)
+    row = lax.broadcasted_iota(jnp.int32, (height, HALF), 0)
+    tiles = [
+        [work[n, pl.ds(i * height, height), :] for i in range(HALF // height)] for n in range(count)
+    ]
+    for p in range(0, HALF, 2):
+        at, r = p // height, p % height
+        first, second = lane == p, lane == p + 1
+        for n in range(count):
+            old = tiles[n]
+            shape = (height, HALF)
+            left = [jnp.broadcast_to(t[:, p : p + 1], shape) for t in old]
+            right = [jnp.broadcast_to(t[:, p + 1 : p + 2], shape) for t in old]
+            a00, a10 = left[at][r : r + 1], left[at][r + 1 : r + 2]
+            a01, a11 = right[at][r : r + 1], right[at][r + 1 : r + 2]
+            over = 1.0 / a00
+            s, t = a01 * over, a10 * over
+            low = 1.0 / (a11 - a10 * s)
+            top0 = jnp.where(first, 1.0, jnp.where(second, 0.0, old[at][r : r + 1]))
+            top1 = jnp.where(first, 0.0, jnp.where(second, 1.0, old[at][r + 1 : r + 2]))
+            w1 = low * (top1 - t * top0)
+            w0 = over * top0 - s * w1
+            left[at] = jnp.where(row == r, -1.0, jnp.where(row == r + 1, 0.0, left[at]))
+            right[at] = jnp.where(row == r, 0.0, jnp.where(row == r + 1, -1.0, right[at]))
+            both = first | second
+            new = []
+            for i, tile in enumerate(old):
+                kept = jnp.where(both, 0.0, tile)
+                if i == at:
+                    kept = jnp.where((row == r) | (row == r + 1), 0.0, kept)
+                new.append(kept - left[i] * w0 - right[i] * w1)
+            tiles[n] = new
+    for n in range(count):
+        for i, tile in enumerate(tiles[n]):
+            work[n, pl.ds(i * height, height), :] = tile
+
+
+def iterate_kernel(
+    m_ref, p_ref, j_ref, t_ref, answer_ref, residual_ref,
+    normal, back, direction, lift, pushed, answer, gram, systems, work, inverse, upper,
+):
+    feat = lax.axis_index("feat")
+    blocks = pairs(Z)
+    for n, (i, j) in enumerate(blocks):
+        rows = slice(i * BLOCK, (i + 1) * BLOCK)
+        if j is None:
+            back[:, rows] = m_ref[n].astype(jnp.float32)
+            continue
+        columns = slice(j * BLOCK, (j + 1) * BLOCK)
+        normal[rows, columns] = m_ref[n]
+        if i != j:
+            normal[columns, rows] = m_ref[n].T
+
+    def gradient():
+        descent = dot(back[...].astype(jnp.bfloat16), p_ref[...], PLAIN)
+        return descent, dot(descent, descent, ACROSS, precise)
+
+    def factor():
+        def step(block, carry):
+            for n in range(2):
+
+                @pl.when(block == 0)
+                def _():
+                    work[n] = systems[n, :HALF, :HALF]
+
+                @pl.when(block == 1)
+                def _():
+                    upper[n] = dot(inverse[0, n], systems[n, :HALF, HALF:], PLAIN, precise)
+                    work[n] = systems[n, HALF:, HALF:] - dot(
+                        systems[n, HALF:, :HALF], upper[n], PLAIN, precise
+                    )
+
+            invert(work, 2)
+            for n in range(2):
+                inverse[block, n] = work[n]
+            return carry
+
+        lax.fori_loop(0, 2, step, 0)
+
+    def solve(n, right):
+        begun = dot(inverse[0, n], right[:HALF], PLAIN, precise)
+        rest = right[HALF:] - dot(systems[n, HALF:, :HALF], begun, PLAIN, precise)
+        lower = dot(inverse[1, n], rest, PLAIN, precise)
+        return jnp.concatenate([begun - dot(upper[n], lower, PLAIN, precise), lower], axis=0)
+
+    descent, first = gradient()
+    direction[...] = descent
+    gram[...] = first
+    answer[...] = jnp.zeros_like(answer)
+
+    def iteration(index, carry):
+        lift[...] = dot(direction[...].astype(jnp.bfloat16), p_ref[...], ACROSS)
+        rounded = lift[...].astype(jnp.bfloat16)
+        pushed[...] = dot(rounded, normal[...], PLAIN)
+        systems[0] = dot(rounded.astype(jnp.float32), pushed[...], ACROSS, precise)
+        systems[1] = gram[...]
+        factor()
+        step_size = solve(0, gram[...]).T
+        answer[...] += dot(step_size, lift[...], PLAIN, precise)
+
+        @pl.when(index + 1 < ITERS)
+        def _():
+            back[...] -= dot(step_size, pushed[...], PLAIN, precise)
+            descent, following = gradient()
+            mixing = solve(1, following).T
+            direction[...] = descent + dot(mixing, direction[...], PLAIN, precise)
+            gram[...] = following
+
+        return carry
+
+    lax.fori_loop(0, ITERS, iteration, 0)
+    fitted = jnp.zeros(residual_ref.shape, jnp.float32)
+    for i in range(Z):
+        fitted += dot(j_ref[i], answer[:, i * BLOCK : (i + 1) * BLOCK].astype(jnp.bfloat16), ACROSS)
+    residual_ref[...] = t_ref[...].astype(jnp.float32) - fitted
+    share = answer_ref.shape[0]
+    answer_ref[...] = answer[:, pl.ds(pl.multiple_of(feat * share, share), share)].T
+
+
+def on_block(activations, down_proj, precond, target):
+    joined, sums = reduced(activations, down_proj.T, target)
+    rank, wanted = precond.shape[0], target.shape[1]
+    f32 = jnp.float32
+    whole = pl.BlockSpec(memory_space=pltpu.VMEM)
+    wide, square, small = (wanted, rank), (wanted, wanted), (2, HALF, HALF)
+    return pl.pallas_call(
+        iterate_kernel,
+        out_shape=(
+            jax.ShapeDtypeStruct((rank // lax.axis_size("feat"), wanted), f32),
+            jax.ShapeDtypeStruct(target.shape, f32),
+        ),
+        in_specs=[whole] * 4,
+        out_specs=(whole, whole),
+        scratch_shapes=[
+            pltpu.VMEM((rank, rank), jnp.bfloat16),
+            pltpu.VMEM(wide, f32),
+            pltpu.VMEM(wide, f32),
+            pltpu.VMEM(wide, f32),
+            pltpu.VMEM(wide, f32),
+            pltpu.VMEM(wide, f32),
+            pltpu.VMEM(square, f32),
+            pltpu.VMEM((2,) + square, f32),
+            pltpu.VMEM(small, f32),
+            pltpu.VMEM((2,) + small, f32),
+            pltpu.VMEM(small, f32),
+        ],
+        compiler_params=pltpu.CompilerParams(vmem_limit_bytes=48 * 2**20),
+    )(sums, precond, joined, target)
+
+
 def solve_gram(matrix, right):
     lower = jnp.linalg.cholesky(matrix)
     middle = lax.linalg.triangular_solve(lower, right, left_side=True, lower=True)
     return lax.linalg.triangular_solve(lower, middle, left_side=True, lower=True, transpose_a=True)
-
-
-def wide_dot(a, b, dims):
-    return lax.dot_general(a, b, (dims, ((), ())), preferred_element_type=jnp.float32)
-
-
-def on_block(activations, down_proj, precond, target):
-    feat_index = lax.axis_index("feat")
-    joined, sums = reduced(activations, down_proj.T, target)
-    blocks = dict(zip(pairs(Z), sums))
-    normal = jnp.concatenate(
-        [
-            jnp.concatenate([blocks[i, j] if i <= j else blocks[j, i].T for j in range(Z)], axis=1)
-            for i in range(Z)
-        ],
-        axis=0,
-    )
-    back = jnp.concatenate([blocks[i, None] for i in range(Z)], axis=0).astype(jnp.float32)
-
-    def gradient(current):
-        descent = wide_dot(precond, current.astype(jnp.bfloat16), ((0,), (0,)))
-        return descent, jnp.dot(descent.T, descent, precision=precise)
-
-    descent, gram_now = gradient(back)
-    direction = descent
-    answer = jnp.zeros(back.shape, jnp.float32)
-    for iteration in range(ITERS):
-        lift = wide_dot(precond, direction.astype(jnp.bfloat16), ((1,), (0,)))
-        rounded = lift.astype(jnp.bfloat16)
-        pushed = wide_dot(normal, rounded, ((1,), (0,)))
-        curvature = jnp.dot(rounded.astype(jnp.float32).T, pushed, precision=precise)
-        curvature = 0.5 * (curvature + curvature.T)
-        step_size = solve_gram(curvature, gram_now)
-        answer = answer + jnp.dot(lift, step_size, precision=precise)
-        if iteration + 1 < ITERS:
-            back = back - jnp.dot(pushed, step_size, precision=precise)
-            descent, gram_next = gradient(back)
-            mixing = solve_gram(gram_now, gram_next)
-            direction = descent + jnp.dot(direction, mixing, precision=precise)
-            gram_now = gram_next
-    rounded = answer.astype(jnp.bfloat16).reshape(Z, BLOCK, -1)
-    fitted = sum(wide_dot(joined[i], rounded[i], ((1,), (0,))) for i in range(Z))
-    share = answer.shape[0] // lax.axis_size("feat")
-    return (
-        lax.dynamic_slice_in_dim(answer, feat_index * share, share, 0),
-        target.astype(jnp.float32) - fitted,
-    )
 
 
 def on_device(activations, down_proj, precond, target):

time: 469 us -> 215 us (0.46); the launches traced: 463 us -> 215 us
  other arithmetic: 200 us -> 0 us
  local copies, waits for them, and re-layouts: 56.1 us -> 2.73 us
  Pallas kernels: 160 us -> 211 us
  matrix products: 41.2 us -> 0 us
  between operations: 5.47 us -> 0.68 us
    another operation x26 -> x0, other arithmetic: 187 us -> none  [the longest x19 119 us: solve_gram(): lower = jnp.linalg.cholesky(matrix)]
    pallas_call x0 -> x1, Pallas kernels: none -> 51.9 us  [on_block(): pl.pallas_call(iterate_kernel, out_shape=(jax.ShapeDtypeStruct((rank // l...]
    another operation x30 -> x0, local copies, waits for them, and re-layouts: 30.8 us -> none  [the longest x22 21.4 us: solve_gram(): lax.linalg.triangular_solve(lower, middle, left_side=True, lower=True, tr...]
    another operation x24 -> x0, matrix products: 23.5 us -> none  [the longest x6 9.67 us: solve_gram(): lower = jnp.linalg.cholesky(matrix)]
    dot_general x18 -> x0, matrix products: 17.7 us -> none  [the longest x10 6.15 us: wide_dot(): lax.dot_general(a, b, (dims, ((), ())), preferred_element_type=jnp.float32)]
    concatenate x2 -> x0, other arithmetic: 6.87 us -> none  [the longest x1 6.04 us: on_block(): jnp.concatenate([jnp.concatenate([blocks[i, j] if i <= j else blocks[j, i...]
where the time goes in v2:
time: 215 us
  Pallas kernels  211 us (98%)
  local copies, waits for them, and re-layouts  2.73 us (1%)
    pallas_call x1, Pallas kernels, reduced(): pl.pallas_call(reduce_kernel, out_shape=(jax.ShapeDtypeStruct((Z, tokens,...  160 us
    pallas_call x1, Pallas kernels, on_block(): pl.pallas_call(iterate_kernel, out_shape=(jax.ShapeDtypeStruct((rank // l...  51.9 us

profile of v2, /device:TPU:0, one launch (start us, length us, event | category | flops | bytes accessed | tf_op | source)
XLA Modules:
  0.0 214.9 jit_solution(4830214714039114620)
XLA Ops:
  0.6 0.0 copy-start
  0.6 0.0 copy-start.3
  0.7 159.5 %shard_map.59 = (bf16[4,512,256]{2,1,0:T(8,128)(2,1)}, bf16[14,256,256]{2,1,0:T(8,128)(2,1)}) custom-call(bf16[512,8192]{1,0:T(8,128)(2,1)} %a_ref.1, bf16[64,8192]{1,0:T(8,128)(2,1)} %bitcast.1, bf16[512,256]{1,0:T(8,128)(2,1)} %t_ref.3), custom_call_target="tpu_custom_call" | custom-call | flops 8589934592 | bytes 8388608 | tf_op jit(solution)/shard_map/pallas_call | solution.py:224
  160.2 0.0 copy-done
  160.2 0.0 copy-done.3
  160.2 0.0 copy-start.1
  160.2 1.5 copy-done.1
  161.7 0.0 copy-start.2
  161.7 1.2 copy-done.2
  162.9 51.9 %shard_map.60 = (f32[512,256]{1,0:T(8,128)}, f32[512,256]{1,0:T(8,128)}) custom-call(bf16[14,256,256]{2,1,0:T(8,128)(2,1)S(1)} %copy-done.1, bf16[1024,1024]{1,0:T(8,128)(2,1)S(1)} %copy-done, bf16[4,512,256]{2,1,0:T(8,128)(2,1)S(1)} %copy-done.2, bf16[512,256]{1,0:T(8,128)(2,1)S(1)} %copy-done.3), custom_call_target="tpu_custom_call" | custom-call | tf_op jit(solution)/shard_map/pallas_call | solution.py:390
Async XLA Ops:
  0.6 159.6 %copy-start = (bf16[1024,1024]{1,0:T(8,128)(2,1)S(1)}, bf16[1024,1024]{1,0:T(8,128)(2,1)}, u32[]{:S(2)}) copy-start(bf16[1024,1024]{1,0:T(8,128)(2,1)} %p_ref.1) | copy-start | bytes 6291460
  0.6 159.6 %copy-start.3 = (bf16[512,256]{1,0:T(8,128)(2,1)S(1)}, bf16[512,256]{1,0:T(8,128)(2,1)}, u32[]{:S(2)}) copy-start(bf16[512,256]{1,0:T(8,128)(2,1)} %t_ref.3) | copy-start | bytes 786436
  160.2 1.5 copy-start.1
  161.7 1.2 copy-start.2

commit v3 on v2

--- a/solution.py
+++ b/solution.py
@@ -15,78 +15,101 @@
 precise = lax.Precision.HIGHEST
 
 
-def spread(buf, send, recv, on_slab):
+def spread(views, side_first, send, recv, on_slab):
     me = lax.axis_index("tok")
     z, y, c = me // (Y * CORES), (me // CORES) % Y, me % CORES
+    parts = range(len(views))
 
     def index(zz, yy, cc):
         return (zz * Y + yy) * CORES + cc
 
     targets = (me + Y * CORES, me - Y * CORES, index(z, 1 - y, c), index(z, y, 1 - c))
 
-    def copy(i, way):
+    def copy(n, i, way):
         return pltpu.make_async_remote_copy(
-            src_ref=buf.at[i],
-            dst_ref=buf.at[i],
-            send_sem=send.at[way, i],
-            recv_sem=recv.at[i],
+            src_ref=views[n](i),
+            dst_ref=views[n](i),
+            send_sem=send.at[n, way, i],
+            recv_sem=recv.at[n, i],
             device_id={"tok": targets[way]},
             device_id_type=MESH,
         )
 
     def along(distance, visit):
-        for sign in (1, -1) if distance else (1,):
+        for sign in (1, -1) if distance else (0,):
             zz = z + sign * distance
 
             @pl.when((zz >= 0) & (zz < Z))
             def _():
                 visit(zz, sign)
 
-    def onward(i, zz, sign, act):
-        if sign != 1 or zz is z:
+    def onward(act, n, i, sign, side):
+        if side:
+            act(copy(n, i, 2))
+        if sign is not None and sign <= 0:
 
             @pl.when(z < Z - 1)
             def _():
-                act(copy(i, 0))
-
-        if sign == 1:
+                act(copy(n, i, 0))
+
+        if sign is not None and sign >= 0:
 
             @pl.when(z > 0)
             def _():
-                act(copy(i, 1))
-
-        act(copy(i, 2))
-        act(copy(i, 3))
-
-    onward(me, z, 1, lambda k: k.start())
+                act(copy(n, i, 1))
+
+        act(copy(n, i, 3))
+
+    def begin(act):
+        for n in parts[::-1]:
+            onward(act, n, me, 0, True)
+
+    def lines(zz, sign, act, arrive):
+        for n in parts:
+            for yy in (y, 1 - y) if side_first[n] else (y,):
+                i = index(zz, yy, c)
+                if arrive is not None:
+                    arrive(copy(n, i, 3))
+                onward(act, n, i, sign, not side_first[n])
+
+    def sides(zz, act, arrive, first):
+        for n in parts:
+            if side_first[n] == first:
+                i = index(zz, 1 - y, c)
+                if arrive is not None:
+                    arrive(copy(n, i, 3))
+                onward(act, n, i, 0 if first else None, False)
+
+    def start(copied):
+        copied.start()
+
+    def arrived(copied):
+        copied.wait_recv()
+
+    def sent(copied):
+        copied.wait_send()
+
+    def slab(zz, sign):
+        for n in parts:
+            for yy in (y, 1 - y):
+                arrived(copy(n, index(zz, yy, 1 - c), 3))
+        if on_slab is not None:
+            on_slab(zz)
+
+    begin(start)
+    sides(z, start, arrived, True)
     for stage in range(Z):
-
-        def line(zz, sign):
-            i = index(zz, y, c)
-            copy(i, 2).wait_recv()
-            onward(i, zz, sign, lambda k: k.start())
-
-        def side(zz, sign):
-            i = index(zz, 1 - y, c)
-            copy(i, 2).wait_recv()
-            copy(i, 3).start()
-
-        def slab(zz, sign):
-            copy(index(zz, y, 1 - c), 3).wait_recv()
-            copy(index(zz, 1 - y, 1 - c), 3).wait_recv()
-            if on_slab is not None:
-                on_slab(zz)
-
         if stage + 1 < Z:
-            along(stage + 1, line)
-        along(stage, side)
+            along(stage + 1, lambda zz, sign: lines(zz, sign, start, arrived))
+        along(stage, lambda zz, sign: sides(zz, start, arrived, False))
         along(stage, slab)
 
-    onward(me, z, 1, lambda k: k.wait_send())
+    begin(sent)
+    sides(z, sent, None, True)
     for stage in range(Z):
-        if stage:
-            along(stage, lambda zz, sign: onward(index(zz, y, c), zz, sign, lambda k: k.wait_send()))
-        along(stage, lambda zz, sign: copy(index(zz, 1 - y, c), 3).wait_send())
+        if stage + 1 < Z:
+            along(stage + 1, lambda zz, sign: lines(zz, sign, sent, None))
+        along(stage, lambda zz, sign: sides(zz, sent, None, False))
 
 
 def pairs(slabs):
@@ -96,8 +119,8 @@
 
 def reduce_kernel(
     a_ref, d_ref, t_ref, j_ref, m_ref,
-    a_buf, d_buf, total, mine, theirs, out_buf, in_buf, all_buf,
-    a_sem, d_sem, d_send, d_recv, x_send, x_recv, r_send, r_recv, p_send, p_recv, m_send, m_recv,
+    a_buf, d_buf, total, mine, theirs, out_buf, core_buf, pair_buf, in_buf, all_buf,
+    a_sem, d_sem, d_send, d_recv, x_send, x_recv, c_send, c_recv, r_send, r_recv, p_send, p_recv, m_send, m_recv,
 ):
     me, feat = lax.axis_index("tok"), lax.axis_index("feat")
     count = Z * Y * CORES
@@ -143,7 +166,12 @@
         swap(slab).start()
 
     load_a.wait()
-    spread(d_buf, d_send, d_recv, project)
+    eighth = d_buf.shape[2] // 8
+    views = [
+        lambda i, low=low, size=size: d_buf.at[i, :, pl.ds(low * eighth, size * eighth)]
+        for low, size in ((0, 3), (3, 4), (7, 1))
+    ]
+    spread(views, (False, False, True), d_send, d_recv, project)
     for slab in range(Z):
         swap(slab).wait()
         j_ref[slab] = (mine[slab].astype(jnp.float32) + theirs[slab].astype(jnp.float32)).astype(
@@ -152,7 +180,7 @@
 
     blocks = pairs(Z)
     half = len(blocks) // 2
-    rows = BLOCK // count
+    rows, chips = BLOCK // count, Z * Y
     for owner in range(2):
 
         @pl.when(feat == owner)
@@ -164,38 +192,44 @@
                     (((0,), (0,)), ((), ())),
                     preferred_element_type=jnp.float32,
                 )
-                out_buf[:, n] = product.astype(jnp.bfloat16).reshape(count, rows, BLOCK)
-
-    def send_part(step):
-        other = lax.rem(me + step, count)
+                out_buf[:, :, n] = product.astype(jnp.bfloat16).reshape(CORES, chips, rows, BLOCK)
+
+    chip, core = me // CORES, me % CORES
+    between = pltpu.make_async_remote_copy(
+        src_ref=out_buf.at[1 - core],
+        dst_ref=core_buf,
+        send_sem=c_send,
+        recv_sem=c_recv,
+        device_id={"tok": chip * CORES + 1 - core},
+        device_id_type=MESH,
+    )
+    between.start()
+    between.wait()
+    for i in range(chips):
+        pair_buf[i] = (out_buf[core, i].astype(jnp.float32) + core_buf[i].astype(jnp.float32)).astype(
+            jnp.bfloat16
+        )
+
+    def part(step, slot, sem):
+        other = lax.rem(chip + step, chips)
         return pltpu.make_async_remote_copy(
-            src_ref=out_buf.at[other],
-            dst_ref=in_buf.at[me],
+            src_ref=pair_buf.at[other],
+            dst_ref=in_buf.at[slot],
             send_sem=r_send.at[step],
-            recv_sem=r_recv.at[me],
-            device_id={"tok": other},
+            recv_sem=r_recv.at[sem],
+            device_id={"tok": other * CORES + core},
             device_id_type=MESH,
         )
 
-    def take_part(step):
-        other = lax.rem(me + step, count)
-        pltpu.make_async_remote_copy(
-            src_ref=out_buf.at[other],
-            dst_ref=in_buf.at[other],
-            send_sem=r_send.at[step],
-            recv_sem=r_recv.at[other],
-            device_id={"tok": other},
-            device_id_type=MESH,
-        ).wait_recv()
-
-    for step in range(1, count):
-        send_part(step).start()
-    in_buf[me] = out_buf[me]
-    for step in range(1, count):
-        take_part(step)
+    for step in range(1, chips):
+        part(step, chip, chip).start()
+    in_buf[chip] = pair_buf[chip]
+    for step in range(1, chips):
+        other = lax.rem(chip + step, chips)
+        part(step, other, other).wait_recv()
     for n in range(half):
         summed = in_buf[0, n].astype(jnp.float32)
-        for i in range(1, count):
+        for i in range(1, chips):
             summed += in_buf[i, n].astype(jnp.float32)
         all_buf[me, feat * half + n] = summed.astype(jnp.bfloat16)
     own = all_buf.at[me, pl.ds(feat * half, half)]
@@ -205,11 +239,12 @@
     )
     across.start()
     across.wait()
-    spread(all_buf, m_send, m_recv, None)
-    for step in range(1, count):
-        send_part(step).wait_send()
+    spread([lambda i: all_buf.at[i]], (False,), m_send, m_recv, None)
+    for step in range(1, chips):
+        part(step, chip, chip).wait_send()
     for i in range(count):
-        m_ref[:, pl.ds(i * rows, rows), :] = all_buf[i]
+        place = (i % CORES) * chips + i // CORES
+        m_ref[:, pl.ds(place * rows, rows), :] = all_buf[i]
 
 
 def reduced(activations, down_rows, target):
@@ -217,7 +252,7 @@
     tokens, features = activations.shape
     share = down_rows.shape[0]
     blocks = len(pairs(Z))
-    half, rows = blocks // 2, BLOCK // count
+    half, rows, chips = blocks // 2, BLOCK // count, Z * Y
     dma = pltpu.SemaphoreType.DMA
     bf16 = jnp.bfloat16
     whole = pl.BlockSpec(memory_space=pltpu.VMEM)
@@ -235,11 +270,13 @@
             pltpu.VMEM((tokens, BLOCK), jnp.float32),
             pltpu.VMEM((Z, tokens, BLOCK), bf16),
             pltpu.VMEM((Z, tokens, BLOCK), bf16),
-            pltpu.VMEM((count, half, rows, BLOCK), bf16),
-            pltpu.VMEM((count, half, rows, BLOCK), bf16),
+            pltpu.VMEM((CORES, chips, half, rows, BLOCK), bf16),
+            pltpu.VMEM((chips, half, rows, BLOCK), bf16),
+            pltpu.VMEM((chips, half, rows, BLOCK), bf16),
+            pltpu.VMEM((chips, half, rows, BLOCK), bf16),
             pltpu.VMEM((count, blocks, rows, BLOCK), bf16),
-            dma, dma, dma((4, count)), dma((count,)), dma((Z,)), dma((Z,)),
-            dma((count,)), dma((count,)), dma, dma, dma((4, count)), dma((count,)),
+            dma, dma, dma((3, 4, count)), dma((3, count)), dma((Z,)), dma((Z,)), dma, dma,
+            dma((chips,)), dma((chips,)), dma, dma, dma((1, 4, count)), dma((1, count)),
         ],
         compiler_params=pltpu.CompilerParams(
             collective_id=0, has_side_effects=True, vmem_limit_bytes=56 * 2**20
@@ -260,21 +297,22 @@
 HALF = BLOCK // 2
 
 
-def invert(work, count):
+def invert(work, scaled, count):
     height = 8
     lane = lax.broadcasted_iota(jnp.int32, (1, HALF), 1)
     row = lax.broadcasted_iota(jnp.int32, (height, HALF), 0)
+    shape = (height, HALF)
     tiles = [
         [work[n, pl.ds(i * height, height), :] for i in range(HALF // height)] for n in range(count)
     ]
     for p in range(0, HALF, 2):
         at, r = p // height, p % height
-        first, second = lane == p, lane == p + 1
+        first, second, done = lane == p, lane == p + 1, lane <= p + 1
+        both = first | second
         for n in range(count):
             old = tiles[n]
-            shape = (height, HALF)
-            left = [jnp.broadcast_to(t[:, p : p + 1], shape) for t in old]
-            right = [jnp.broadcast_to(t[:, p + 1 : p + 2], shape) for t in old]
+            left = {i: jnp.broadcast_to(old[i][:, p : p + 1], shape) for i in range(at, len(old))}
+            right = {i: jnp.broadcast_to(old[i][:, p + 1 : p + 2], shape) for i in range(at, len(old))}
             a00, a10 = left[at][r : r + 1], left[at][r + 1 : r + 2]
             a01, a11 = right[at][r : r + 1], right[at][r + 1 : r + 2]
             over = 1.0 / a00
@@ -284,24 +322,24 @@
             top1 = jnp.where(first, 0.0, jnp.where(second, 1.0, old[at][r + 1 : r + 2]))
             w1 = low * (top1 - t * top0)
             w0 = over * top0 - s * w1
-            left[at] = jnp.where(row == r, -1.0, jnp.where(row == r + 1, 0.0, left[at]))
-            right[at] = jnp.where(row == r, 0.0, jnp.where(row == r + 1, -1.0, right[at]))
-            both = first | second
-            new = []
-            for i, tile in enumerate(old):
-                kept = jnp.where(both, 0.0, tile)
-                if i == at:
-                    kept = jnp.where((row == r) | (row == r + 1), 0.0, kept)
-                new.append(kept - left[i] * w0 - right[i] * w1)
+            work[n, p : p + 1, :] = jnp.where(done, top0, 0.0)
+            work[n, p + 1 : p + 2, :] = jnp.where(done, top1, 0.0)
+            scaled[n, p : p + 1, :] = jnp.where(done, w0, 0.0)
+            scaled[n, p + 1 : p + 2, :] = jnp.where(done, w1, 0.0)
+            new = list(old)
+            for i in range(at, len(old)):
+                if i == at and r + 2 == height:
+                    continue
+                changed = jnp.where(both, 0.0, old[i]) - left[i] * w0 - right[i] * w1
+                new[i] = jnp.where(row > r + 1, changed, old[i]) if i == at else changed
             tiles[n] = new
     for n in range(count):
-        for i, tile in enumerate(tiles[n]):
-            work[n, pl.ds(i * height, height), :] = tile
+        work[n] = dot(work[n], scaled[n], ((0,), (0,)), precise)
 
 
 def iterate_kernel(
     m_ref, p_ref, j_ref, t_ref, answer_ref, residual_ref,
-    normal, back, direction, lift, pushed, answer, gram, systems, work, inverse, upper,
+    normal, back, direction, lift, pushed, answer, gram, systems, work, scaled, inverse, upper,
 ):
     feat = lax.axis_index("feat")
     blocks = pairs(Z)
@@ -319,9 +357,9 @@
         descent = dot(back[...].astype(jnp.bfloat16), p_ref[...], PLAIN)
         return descent, dot(descent, descent, ACROSS, precise)
 
-    def factor():
+    def factor(count):
         def step(block, carry):
-            for n in range(2):
+            for n in range(count):
 
                 @pl.when(block == 0)
                 def _():
@@ -334,8 +372,8 @@
                         systems[n, HALF:, :HALF], upper[n], PLAIN, precise
                     )
 
-            invert(work, 2)
-            for n in range(2):
+            invert(work, scaled, count)
+            for n in range(count):
                 inverse[block, n] = work[n]
             return carry
 
@@ -352,27 +390,23 @@
     gram[...] = first
     answer[...] = jnp.zeros_like(answer)
 
-    def iteration(index, carry):
+    for index in range(ITERS):
+        last = index + 1 == ITERS
         lift[...] = dot(direction[...].astype(jnp.bfloat16), p_ref[...], ACROSS)
         rounded = lift[...].astype(jnp.bfloat16)
         pushed[...] = dot(rounded, normal[...], PLAIN)
         systems[0] = dot(rounded.astype(jnp.float32), pushed[...], ACROSS, precise)
         systems[1] = gram[...]
-        factor()
+        factor(1 if last else 2)
         step_size = solve(0, gram[...]).T
         answer[...] += dot(step_size, lift[...], PLAIN, precise)
-
-        @pl.when(index + 1 < ITERS)
-        def _():
+        if not last:
             back[...] -= dot(step_size, pushed[...], PLAIN, precise)
             descent, following = gradient()
             mixing = solve(1, following).T
             direction[...] = descent + dot(mixing, direction[...], PLAIN, precise)
             gram[...] = following
 
-        return carry
-
-    lax.fori_loop(0, ITERS, iteration, 0)
     fitted = jnp.zeros(residual_ref.shape, jnp.float32)
     for i in range(Z):
         fitted += dot(j_ref[i], answer[:, i * BLOCK : (i + 1) * BLOCK].astype(jnp.bfloat16), ACROSS)
@@ -405,6 +439,7 @@
             pltpu.VMEM(square, f32),
             pltpu.VMEM((2,) + square, f32),
             pltpu.VMEM(small, f32),
+            pltpu.VMEM(small, f32),
             pltpu.VMEM((2,) + small, f32),
             pltpu.VMEM(small, f32),
         ],

time: 215 us -> 198 us (0.921)
  Pallas kernels: 211 us -> 195 us
    pallas_call x1, Pallas kernels: 160 us -> 143 us  [reduced(): pl.pallas_call(reduce_kernel, out_shape=(jax.ShapeDtypeStruct((Z, tokens,...]
where the time goes in v3:
time: 198 us
  Pallas kernels  195 us (98%)
  local copies, waits for them, and re-layouts  2.73 us (1%)
    pallas_call x1, Pallas kernels, reduced(): pl.pallas_call(reduce_kernel, out_shape=(jax.ShapeDtypeStruct((Z, tokens,...  143 us
    pallas_call x1, Pallas kernels, on_block(): pl.pallas_call(iterate_kernel, out_shape=(jax.ShapeDtypeStruct((rank // l...  51.5 us

profile of v3, /device:TPU:0, one launch (start us, length us, event | category | flops | bytes accessed | tf_op | source)
XLA Modules:
  0.0 198.0 jit_solution(4450113241722791441)
XLA Ops:
  0.6 0.0 copy-start
  0.6 0.0 copy-start.3
  0.7 143.1 %shard_map.59 = (bf16[4,512,256]{2,1,0:T(8,128)(2,1)}, bf16[14,256,256]{2,1,0:T(8,128)(2,1)}) custom-call(bf16[512,8192]{1,0:T(8,128)(2,1)} %a_ref.1, bf16[64,8192]{1,0:T(8,128)(2,1)} %bitcast.1, bf16[512,256]{1,0:T(8,128)(2,1)} %t_ref.3), custom_call_target="tpu_custom_call" | custom-call | flops 8589934592 | bytes 8388608 | tf_op jit(solution)/shard_map/pallas_call | solution.py:259
  143.8 0.0 copy-done
  143.8 0.0 copy-done.3
  143.8 0.0 copy-start.1
  143.8 1.5 copy-done.1
  145.3 0.0 copy-start.2
  145.3 1.2 copy-done.2
  146.5 51.5 %shard_map.60 = (f32[512,256]{1,0:T(8,128)}, f32[512,256]{1,0:T(8,128)}) custom-call(bf16[14,256,256]{2,1,0:T(8,128)(2,1)S(1)} %copy-done.1, bf16[1024,1024]{1,0:T(8,128)(2,1)S(1)} %copy-done, bf16[4,512,256]{2,1,0:T(8,128)(2,1)S(1)} %copy-done.2, bf16[512,256]{1,0:T(8,128)(2,1)S(1)} %copy-done.3), custom_call_target="tpu_custom_call" | custom-call | tf_op jit(solution)/shard_map/pallas_call | solution.py:424
Async XLA Ops:
  0.6 143.1 %copy-start = (bf16[1024,1024]{1,0:T(8,128)(2,1)S(1)}, bf16[1024,1024]{1,0:T(8,128)(2,1)}, u32[]{:S(2)}) copy-start(bf16[1024,1024]{1,0:T(8,128)(2,1)} %p_ref.1) | copy-start | bytes 6291460
  0.6 143.1 %copy-start.3 = (bf16[512,256]{1,0:T(8,128)(2,1)S(1)}, bf16[512,256]{1,0:T(8,128)(2,1)}, u32[]{:S(2)}) copy-start(bf16[512,256]{1,0:T(8,128)(2,1)} %t_ref.3) | copy-start | bytes 786436
  143.8 1.5 copy-start.1
  145.3 1.2 copy-start.2

commit v4 on v3

--- a/solution.py
+++ b/solution.py
@@ -297,44 +297,71 @@
 HALF = BLOCK // 2
 
 
+def added(terms):
+    while len(terms) > 1:
+        terms = [sum(terms[i : i + 2]) for i in range(0, len(terms), 2)]
+    return terms[0]
+
+
+def invert_block(columns, row):
+    columns = list(columns)
+    for q in range(0, len(columns), 2):
+        a, b = columns[q], columns[q + 1]
+        a00, a10, a01, a11 = a[q : q + 1], a[q + 1 : q + 2], b[q : q + 1], b[q + 1 : q + 2]
+        over = 1.0 / (a00 * a11 - a01 * a10)
+        i00, i01, i10, i11 = a11 * over, -a01 * over, -a10 * over, a00 * over
+        for k, column in enumerate(columns):
+            if k == q:
+                f0, f1, rest = i00, i10, 0.0
+            elif k == q + 1:
+                f0, f1, rest = i01, i11, 0.0
+            else:
+                x0, x1 = column[q : q + 1], column[q + 1 : q + 2]
+                f0, f1, rest = i00 * x0 + i01 * x1, i10 * x0 + i11 * x1, column
+            rest = rest - (a * f0 + b * f1)
+            columns[k] = jnp.where(row == q, f0, jnp.where(row == q + 1, f1, rest))
+    return columns
+
+
 def invert(work, scaled, count):
     height = 8
-    lane = lax.broadcasted_iota(jnp.int32, (1, HALF), 1)
-    row = lax.broadcasted_iota(jnp.int32, (height, HALF), 0)
     shape = (height, HALF)
-    tiles = [
-        [work[n, pl.ds(i * height, height), :] for i in range(HALF // height)] for n in range(count)
-    ]
-    for p in range(0, HALF, 2):
-        at, r = p // height, p % height
-        first, second, done = lane == p, lane == p + 1, lane <= p + 1
-        both = first | second
+    lane = lax.broadcasted_iota(jnp.int32, shape, 1)
+    row = lax.broadcasted_iota(jnp.int32, shape, 0)
+    square = (HALF, HALF)
+    diagonal = lax.broadcasted_iota(jnp.int32, square, 0) == lax.broadcasted_iota(jnp.int32, square, 1)
+    scales, tiles = [], []
+    for n in range(count):
+        only = jnp.where(diagonal, work[n], 0.0)
+        across = lax.rsqrt(jnp.sum(only, axis=0, keepdims=True))
+        down = lax.rsqrt(jnp.sum(only, axis=1, keepdims=True))
+        scales.append((across, down))
+        unit = work[n] * across * down
+        tiles.append([unit[i : i + height] for i in range(0, HALF, height)])
+    for at in range(HALF // height):
+        base = at * height
+        panel, done = (lane >= base) & (lane < base + height), lane < base + height
         for n in range(count):
             old = tiles[n]
-            left = {i: jnp.broadcast_to(old[i][:, p : p + 1], shape) for i in range(at, len(old))}
-            right = {i: jnp.broadcast_to(old[i][:, p + 1 : p + 2], shape) for i in range(at, len(old))}
-            a00, a10 = left[at][r : r + 1], left[at][r + 1 : r + 2]
-            a01, a11 = right[at][r : r + 1], right[at][r + 1 : r + 2]
-            over = 1.0 / a00
-            s, t = a01 * over, a10 * over
-            low = 1.0 / (a11 - a10 * s)
-            top0 = jnp.where(first, 1.0, jnp.where(second, 0.0, old[at][r : r + 1]))
-            top1 = jnp.where(first, 0.0, jnp.where(second, 1.0, old[at][r + 1 : r + 2]))
-            w1 = low * (top1 - t * top0)
-            w0 = over * top0 - s * w1
-            work[n, p : p + 1, :] = jnp.where(done, top0, 0.0)
-            work[n, p + 1 : p + 2, :] = jnp.where(done, top1, 0.0)
-            scaled[n, p : p + 1, :] = jnp.where(done, w0, 0.0)
-            scaled[n, p + 1 : p + 2, :] = jnp.where(done, w1, 0.0)
-            new = list(old)
-            for i in range(at, len(old)):
-                if i == at and r + 2 == height:
-                    continue
-                changed = jnp.where(both, 0.0, old[i]) - left[i] * w0 - right[i] * w1
-                new[i] = jnp.where(row > r + 1, changed, old[i]) if i == at else changed
-            tiles[n] = new
+            columns = {
+                i: [jnp.broadcast_to(old[i][:, base + q : base + q + 1], shape) for q in range(height)]
+                for i in range(at, len(old))
+            }
+            block = invert_block(columns[at], row)
+            top = jnp.where(lane == base + row, 1.0, jnp.where(panel, 0.0, old[at]))
+            left = added([block[q] * top[q : q + 1] for q in range(height)])
+            work[n, pl.ds(base, height), :] = jnp.where(done, top, 0.0)
+            scaled[n, pl.ds(base, height), :] = jnp.where(done, left, 0.0)
+            tiles[n] = [
+                jnp.where(panel, 0.0, old[i])
+                - added([columns[i][q] * left[q : q + 1] for q in range(height)])
+                if i > at
+                else old[i]
+                for i in range(len(old))
+            ]
     for n in range(count):
-        work[n] = dot(work[n], scaled[n], ((0,), (0,)), precise)
+        across, down = scales[n]
+        work[n] = dot(work[n], scaled[n], ((0,), (0,)), precise) * across * down
 
 
 def iterate_kernel(

time: 198 us -> 187 us (0.944)
  Pallas kernels: 195 us -> 183 us
    pallas_call x1, Pallas kernels: 51.5 us -> 40.1 us  [on_block(): pl.pallas_call(iterate_kernel, out_shape=(jax.ShapeDtypeStruct((rank // l...]
where the time goes in v4:
time: 187 us
  Pallas kernels  183 us (98%)
  local copies, waits for them, and re-layouts  2.73 us (1%)
    pallas_call x1, Pallas kernels, reduced(): pl.pallas_call(reduce_kernel, out_shape=(jax.ShapeDtypeStruct((Z, tokens,...  143 us
    pallas_call x1, Pallas kernels, on_block(): pl.pallas_call(iterate_kernel, out_shape=(jax.ShapeDtypeStruct((rank // l...  40.1 us

profile of v4, /device:TPU:0, one launch (start us, length us, event | category | flops | bytes accessed | tf_op | source)
XLA Modules:
  0.0 186.6 jit_solution(8070635242828854047)
XLA Ops:
  0.6 0.0 copy-start
  0.6 0.0 copy-start.3
  0.7 143.1 %shard_map.59 = (bf16[4,512,256]{2,1,0:T(8,128)(2,1)}, bf16[14,256,256]{2,1,0:T(8,128)(2,1)}) custom-call(bf16[512,8192]{1,0:T(8,128)(2,1)} %a_ref.1, bf16[64,8192]{1,0:T(8,128)(2,1)} %bitcast.1, bf16[512,256]{1,0:T(8,128)(2,1)} %t_ref.3), custom_call_target="tpu_custom_call" | custom-call | flops 8589934592 | bytes 8388608 | tf_op jit(solution)/shard_map/pallas_call | solution.py:259
  143.8 0.0 copy-done
  143.8 0.0 copy-done.3
  143.8 0.0 copy-start.1
  143.8 1.5 copy-done.1
  145.3 0.0 copy-start.2
  145.3 1.2 copy-done.2
  146.5 40.1 %shard_map.60 = (f32[512,256]{1,0:T(8,128)}, f32[512,256]{1,0:T(8,128)}) custom-call(bf16[14,256,256]{2,1,0:T(8,128)(2,1)S(1)} %copy-done.1, bf16[1024,1024]{1,0:T(8,128)(2,1)S(1)} %copy-done, bf16[4,512,256]{2,1,0:T(8,128)(2,1)S(1)} %copy-done.2, bf16[512,256]{1,0:T(8,128)(2,1)S(1)} %copy-done.3), custom_call_target="tpu_custom_call" | custom-call | tf_op jit(solution)/shard_map/pallas_call | solution.py:451
Async XLA Ops:
  0.6 143.1 %copy-start = (bf16[1024,1024]{1,0:T(8,128)(2,1)S(1)}, bf16[1024,1024]{1,0:T(8,128)(2,1)}, u32[]{:S(2)}) copy-start(bf16[1024,1024]{1,0:T(8,128)(2,1)} %p_ref.1) | copy-start | bytes 6291460
  0.6 143.1 %copy-start.3 = (bf16[512,256]{1,0:T(8,128)(2,1)S(1)}, bf16[512,256]{1,0:T(8,128)(2,1)}, u32[]{:S(2)}) copy-start(bf16[512,256]{1,0:T(8,128)(2,1)} %t_ref.3) | copy-start | bytes 786436
  143.8 1.5 copy-start.1
  145.3 1.2 copy-start.2

commit v5 on v4

--- a/solution.py
+++ b/solution.py
@@ -169,9 +169,9 @@
     eighth = d_buf.shape[2] // 8
     views = [
         lambda i, low=low, size=size: d_buf.at[i, :, pl.ds(low * eighth, size * eighth)]
-        for low, size in ((0, 3), (3, 4), (7, 1))
+        for low, size in ((0, 3), (3, 2), (5, 2), (7, 1))
     ]
-    spread(views, (False, False, True), d_send, d_recv, project)
+    spread(views, (False, False, False, True), d_send, d_recv, project)
     for slab in range(Z):
         swap(slab).wait()
         j_ref[slab] = (mine[slab].astype(jnp.float32) + theirs[slab].astype(jnp.float32)).astype(
@@ -275,7 +275,7 @@
             pltpu.VMEM((chips, half, rows, BLOCK), bf16),
             pltpu.VMEM((chips, half, rows, BLOCK), bf16),
             pltpu.VMEM((count, blocks, rows, BLOCK), bf16),
-            dma, dma, dma((3, 4, count)), dma((3, count)), dma((Z,)), dma((Z,)), dma, dma,
+            dma, dma, dma((4, 4, count)), dma((4, count)), dma((Z,)), dma((Z,)), dma, dma,
             dma((chips,)), dma((chips,)), dma, dma, dma((1, 4, count)), dma((1, count)),
         ],
         compiler_params=pltpu.CompilerParams(
@@ -366,9 +366,11 @@
 
 def iterate_kernel(
     m_ref, p_ref, j_ref, t_ref, answer_ref, residual_ref,
-    normal, back, direction, lift, pushed, answer, gram, systems, work, scaled, inverse, upper,
+    normal, back, direction, lift, pushed, answer, gram, systems, work, scaled, inverse, upper, j_buf, j_sem,
 ):
     feat = lax.axis_index("feat")
+    load_j = pltpu.make_async_copy(j_ref, j_buf, j_sem)
+    load_j.start()
     blocks = pairs(Z)
     for n, (i, j) in enumerate(blocks):
         rows = slice(i * BLOCK, (i + 1) * BLOCK)
@@ -434,9 +436,10 @@
             direction[...] = descent + dot(mixing, direction[...], PLAIN, precise)
             gram[...] = following
 
+    load_j.wait()
     fitted = jnp.zeros(residual_ref.shape, jnp.float32)
     for i in range(Z):
-        fitted += dot(j_ref[i], answer[:, i * BLOCK : (i + 1) * BLOCK].astype(jnp.bfloat16), ACROSS)
+        fitted += dot(j_buf[i], answer[:, i * BLOCK : (i + 1) * BLOCK].astype(jnp.bfloat16), ACROSS)
     residual_ref[...] = t_ref[...].astype(jnp.float32) - fitted
     share = answer_ref.shape[0]
     answer_ref[...] = answer[:, pl.ds(pl.multiple_of(feat * share, share), share)].T
@@ -454,7 +457,7 @@
             jax.ShapeDtypeStruct((rank // lax.axis_size("feat"), wanted), f32),
             jax.ShapeDtypeStruct(target.shape, f32),
         ),
-        in_specs=[whole] * 4,
+        in_specs=[whole, whole, pl.BlockSpec(memory_space=pl.ANY), whole],
         out_specs=(whole, whole),
         scratch_shapes=[
             pltpu.VMEM((rank, rank), jnp.bfloat16),
@@ -469,6 +472,8 @@
             pltpu.VMEM(small, f32),
             pltpu.VMEM((2,) + small, f32),
             pltpu.VMEM(small, f32),
+            pltpu.VMEM(joined.shape, joined.dtype),
+            pltpu.SemaphoreType.DMA,
         ],
         compiler_params=pltpu.CompilerParams(vmem_limit_bytes=48 * 2**20),
     )(sums, precond, joined, target)

time: 187 us -> 188 us (level)
  no operation moved by 1% of the time
where the time goes in v5:
time: 188 us
  Pallas kernels  184 us (98%)
  local copies, waits for them, and re-layouts  2.73 us (1%)
    pallas_call x1, Pallas kernels, reduced(): pl.pallas_call(reduce_kernel, out_shape=(jax.ShapeDtypeStruct((Z, tokens,...  144 us
    pallas_call x1, Pallas kernels, on_block(): pl.pallas_call(iterate_kernel, out_shape=(jax.ShapeDtypeStruct((rank // l...  40.2 us

profile of v5, /device:TPU:0, one launch (start us, length us, event | category | flops | bytes accessed | tf_op | source)
XLA Modules:
  0.0 187.6 jit_solution(15793646086293549266)
XLA Ops:
  0.6 0.0 copy-start
  0.6 0.0 copy-start.3
  0.7 143.8 %shard_map.59 = (bf16[4,512,256]{2,1,0:T(8,128)(2,1)}, bf16[14,256,256]{2,1,0:T(8,128)(2,1)}) custom-call(bf16[512,8192]{1,0:T(8,128)(2,1)} %a_ref.1, bf16[64,8192]{1,0:T(8,128)(2,1)} %bitcast.1, bf16[512,256]{1,0:T(8,128)(2,1)} %t_ref.3), custom_call_target="tpu_custom_call" | custom-call | flops 8589934592 | bytes 8388608 | tf_op jit(solution)/shard_map/pallas_call | solution.py:259
  144.5 0.0 copy-done
  144.5 0.0 copy-done.3
  144.5 0.0 copy-start.1
  144.5 1.5 copy-done.1
  146.0 0.0 copy-start.2
  146.0 1.2 copy-done.2
  147.2 40.2 %shard_map.60 = (f32[512,256]{1,0:T(8,128)}, f32[512,256]{1,0:T(8,128)}) custom-call(bf16[14,256,256]{2,1,0:T(8,128)(2,1)S(1)} %copy-done.1, bf16[1024,1024]{1,0:T(8,128)(2,1)S(1)} %copy-done, bf16[4,512,256]{2,1,0:T(8,128)(2,1)S(1)} %copy-done.2, bf16[512,256]{1,0:T(8,128)(2,1)S(1)} %copy-done.3), custom_call_target="tpu_custom_call" | custom-call | tf_op jit(solution)/shard_map/pallas_call | solution.py:454
Async XLA Ops:
  0.6 143.9 %copy-start = (bf16[1024,1024]{1,0:T(8,128)(2,1)S(1)}, bf16[1024,1024]{1,0:T(8,128)(2,1)}, u32[]{:S(2)}) copy-start(bf16[1024,1024]{1,0:T(8,128)(2,1)} %p_ref.1) | copy-start | bytes 6291460
  0.6 143.9 %copy-start.3 = (bf16[512,256]{1,0:T(8,128)(2,1)S(1)}, bf16[512,256]{1,0:T(8,128)(2,1)}, u32[]{:S(2)}) copy-start(bf16[512,256]{1,0:T(8,128)(2,1)} %t_ref.3) | copy-start | bytes 786436
  144.5 1.5 copy-start.1
  146.0 1.2 copy-start.2
